TPU v7x, 256 devices: a whole 4x4x8 slice. The times are simulated.
256 devices in a mesh: shard: 64 (over y_lo, z, x), node: 4 (over y_hi, core).
Axes of the slice: x: 4, y: 4 (y_hi: 2, y_lo: 2; y = y_hi * 2 + y_lo), z: 8, core: 2. Of those that a mesh axis runs over, the one named last changes fastest.
Arguments:
- inputs: bfloat16 [2, 32768, 8192], P(None, ('shard', 'node')), may hold values from -24 to 24
- key_weight: bfloat16 [8192, 512], P(('node', 'shard')), may hold values from -0.0625 to 0.0625
- key_cotangent: bfloat16 [2, 32768, 512], P(None, ('shard', 'node')), may hold values from -12 to 12
Outputs:
- key_out: bfloat16 [2, 32768, 512], P(None, ('shard', 'node'))
- input_grad: bfloat16 [2, 32768, 8192], P(None, ('shard', 'node'))
- weight_grad: float32 [8192, 512], P(('node', 'shard'))
All inputs are finite; a program needn't handle non-finite values.
Results may differ from a plain program's by a relative error of at most 0.001.
Values may be sent and summed in bfloat16 or wider, within the bound.
A program may use at most 128 MiB of HBM per device.

v0:
```python
import jax
import jax.numpy as jnp
from jax import lax
from jax.sharding import PartitionSpec as P


def local(inputs, key_weight, key_cotangent):
    batches, tokens_dev, feature_dim = inputs.shape
    key_width = key_weight.shape[1]
    token_rows = inputs.reshape(batches * tokens_dev, feature_dim)
    cotangent = key_cotangent.reshape(batches * tokens_dev, key_width)
    secondary = lax.all_gather(key_weight, "shard", axis=0, tiled=True)
    columns = token_rows
    key_full = jnp.dot(
        columns,
        lax.all_gather(secondary, "node", axis=0, tiled=True),
        preferred_element_type=jnp.float32,
    )
    back_full = lax.dot_general(
        cotangent,
        lax.all_gather(secondary, "node", axis=0, tiled=True),
        (((1,), (1,)), ((), ())),
        preferred_element_type=jnp.float32,
    )
    node_count = lax.axis_size("node")
    shard_count = lax.axis_size("shard")
    columns = token_rows
    partial_value = lax.psum_scatter(
        lax.dot_general(
            columns, cotangent, (((0,), (0,)), ((), ())), preferred_element_type=jnp.float32
        ),
        "node",
        scatter_dimension=0,
        tiled=True,
    )
    summed = lax.psum_scatter(partial_value, "shard", scatter_dimension=0, tiled=True)
    factor = float(batches * tokens_dev * node_count * shard_count) ** (-0.5)
    key_out = key_full.astype(jnp.bfloat16).reshape(batches, tokens_dev, key_width)
    input_grad = back_full.astype(jnp.bfloat16).reshape(batches, tokens_dev, feature_dim)
    return (key_out, input_grad, summed * factor)


def solution(mesh):
    in_specs = (
        P(None, ("shard", "node"), None),
        P(("node", "shard"), None),
        P(None, ("shard", "node"), None),
    )
    out_specs = (
        P(None, ("shard", "node"), None),
        P(None, ("shard", "node"), None),
        P(("node", "shard"), None),
    )
    return jax.shard_map(local, mesh=mesh, in_specs=in_specs, out_specs=out_specs, check_vma=False)
```

profile of v0, /device:TPU:8, one launch (start us, length us, event | category | flops | bytes accessed | tf_op | source)
XLA Modules:
  0.0 646.8 jit_solution(560421204996340952)
XLA Ops:
  8.0 0.0 copy-start
  8.0 0.0 all-gather.3.cloned.1.call-start
  8.1 0.7 all-gather.3.cloned.1.call-update
  8.7 0.0 reduce-scatter.3.cloned.1.call-start
  8.8 0.2 copy-done
  9.0 10.3 %convolution_bitcast_fusion = f32[8192,512]{1,0:T(8,128)} fusion(bf16[2,128,8192]{2,1,0:T(8,128)(2,1)} %param.3, bf16[2,128,512]{2,1,0:T(8,128)(2,1)S(1)} %copy-done), kind=kOutput, calls=%fused_computation | convolution fusion | flops 2147483648 | bytes 21233664 | tf_op jit(solution)/shard_map/dot_general | solution.py:29
  19.3 0.0 reduce-scatter.3.cloned.1.call-update
  19.3 0.0 all-gather.5.cloned.1.call-start
  19.3 294.3 %all-gather.3.cloned.1.call-done = bf16[2048,512]{1,0:T(8,128)(2,1)} async-done(((bf16[32,512]{1,0:T(8,128)(2,1)}), bf16[2048,512]{1,0:T(8,128)(2,1)}) %all-gather.3.cloned.1.call-update) | async-done | bytes 2097168 | tf_op jit(solution)/shard_map/all_gather | solution.py:12
  313.6 0.0 all-gather.5.cloned.1.call-update
  313.6 0.0 reduce-scatter.5.cloned.1.call-start
  313.7 0.0 reduce-scatter.3.cloned.1.call-done
  313.7 0.7 reduce-scatter.5.cloned.1.call-update
  314.4 69.6 %all-gather.5.cloned.1.call-done = bf16[8192,512]{1,0:T(8,128)(2,1)} async-done(((bf16[2048,512]{1,0:T(8,128)(2,1)}), bf16[8192,512]{1,0:T(8,128)(2,1)}) %all-gather.5.cloned.1.call-update) | async-done | bytes 8388624 | tf_op jit(solution)/shard_map/all_gather | solution.py:16
  383.9 0.0 copy-start.1
  383.9 0.0 copy-start.2
  383.9 8.0 %convolution_convert_fusion = bf16[256,8192]{1,0:T(8,128)(2,1)} fusion(bf16[256,512]{1,0:T(8,128)(2,1)S(1)} %bitcast.12, bf16[8192,512]{1,0:T(8,128)(2,1)} %all-gather.5.cloned.1.call-done), kind=kOutput, calls=%fused_computation.1 | convolution fusion | flops 2149580800 | bytes 12845056 | tf_op jit(solution)/shard_map/dot_general | solution.py:19
  391.9 0.0 copy-done.1
  391.9 0.0 copy-done.2
  391.9 3.0 convolution_convert_fusion.1
  394.9 242.9 %reduce-scatter.5.cloned.1.call-done = f32[32,512]{1,0:T(8,128)} async-done(((f32[2048,512]{1,0:T(8,128)}), f32[32,512]{1,0:T(8,128)}) %reduce-scatter.5.cloned.1.call-update) | async-done | bytes 65552 | tf_op jit(solution)/shard_map/reduce_scatter | solution.py:36
  637.9 1.5 broadcast_multiply_fusion
Async XLA Ops:
  8.0 1.0 copy-start
  8.0 305.6 %all-gather.3.cloned.1.call-start = ((), (), s32[]{:S(2)}) async-start(), calls=%async_computation.2 | async-start | bytes 2129920 | tf_op jit(solution)/shard_map/all_gather | solution.py:12
  8.7 305.0 %reduce-scatter.3.cloned.1.call-start = ((), (), s32[]{:S(2)}) async-start(), calls=%async_computation.4 | async-start | bytes 20971520 | tf_op jit(solution)/shard_map/reduce_scatter | solution.py:28
  19.3 364.7 %all-gather.5.cloned.1.call-start = ((), (), s32[]{:S(2)}) async-start(), calls=%async_computation.3 | async-start | bytes 10485760 | tf_op jit(solution)/shard_map/all_gather | solution.py:16
  313.6 324.2 %reduce-scatter.5.cloned.1.call-start = ((), (), s32[]{:S(2)}) async-start(), calls=%async_computation.5 | async-start | bytes 4259840 | tf_op jit(solution)/shard_map/reduce_scatter | solution.py:36
  383.9 8.0 %copy-start.1 = (bf16[2,128,8192]{2,1,0:T(8,128)(2,1)S(1)}, bf16[2,128,8192]{2,1,0:T(8,128)(2,1)}, u32[]{:S(2)}) copy-start(bf16[2,128,8192]{2,1,0:T(8,128)(2,1)} %param.3) | copy-start | bytes 12582916
  383.9 8.0 %copy-start.2 = (bf16[8192,512]{1,0:T(8,128)(2,1)S(1)}, bf16[8192,512]{1,0:T(8,128)(2,1)}, u32[]{:S(2)}) copy-start(bf16[8192,512]{1,0:T(8,128)(2,1)} %all-gather.5.cloned.1.call-done) | copy-start | bytes 25165828
Sparse Core Ops, SparseCore 0:
  10.8 302.7 all-gather.2
  317.1 320.6 reduce-scatter.4
Sparse Core Ops, SparseCore 1:
  19.4 148.4 reduce-scatter.2
  313.7 70.2 all-gather.4
where the time goes:
time: 647 us
  waiting for transfers between devices  608 us (94%)
  matrix products  21.3 us (3%)
  between operations  15.5 us (2%)
    all_gather x1, waiting for transfers between devices, local(): secondary = lax.all_gather(key_weight, 'shard', axis=0, tiled=True)  294 us
    reduce_scatter x1, waiting for transfers between devices, local(): lax.psum_scatter(partial_value, 'shard', scatter_dimension=0, tiled=True)  243 us
    all_gather x1, waiting for transfers between devices, local(): lax.all_gather(secondary, 'node', axis=0, tiled=True)  69.6 us
  transfers between devices with their start and end apart: 4, of which 3 were waited for; matrix products, arithmetic and copies ran while one was open for 3% of the time, Pallas kernels for 0%

commit v1 on v0

v1 whole, which is shorter than its diff:
```python
import jax
import jax.numpy as jnp
from jax import lax
from jax.experimental import pallas as pl
from jax.experimental.pallas import tpu as pltpu
from jax.sharding import PartitionSpec as P

MESH = pl.DeviceIdType.MESH
F32 = jnp.float32
BF16 = jnp.bfloat16
ALL = slice(None)

NX, NY, NZ = 4, 4, 8
ROWS = 32


def place():
    s = lax.axis_index("shard")
    n = lax.axis_index("node")
    x = lax.rem(s, NX)
    z = lax.rem(s // NX, NZ)
    y = (n // 2) * 2 + s // (NX * NZ)
    return x, y, z, lax.rem(n, 2)


def device(x, y, z, c):
    return (lax.rem(y, 2) * (NX * NZ) + z * NX + x, (y // 2) * 2 + c)


PART_A = (pl.ds(0, 16), pl.ds(0, 384))
PART_B = (pl.ds(16, 16), pl.ds(0, 384))
PART_AB = (pl.ds(0, 32), pl.ds(0, 384))
PART_C = (pl.ds(0, 32), pl.ds(384, 128))

SEMS = 128


def kernel(inputs, weight, cot, key_out, input_grad, weight_grad,
           xs, cs, ws, grad, acc, key_in, stage,
           ra1, rb1, rc1, ra2, rb2, rc2, rab3, rc3,
           send, recv, local):
    x, y, z, c = place()
    factor = 1.0 / 256.0
    counter = [0]
    started = []

    def px(k):
        return lax.rem(x + k + 4 * NX, NX)

    def py(k):
        return lax.rem(y + k + 4 * NY, NY)

    def pz(k):
        return lax.rem(z + k + 4 * NZ, NZ)

    def to(axis, k):
        if axis == "x":
            return device(px(k), y, z, c)
        if axis == "y":
            return device(x, py(k), z, c)
        if axis == "z":
            return device(x, y, pz(k), c)
        return device(x, y, z, 1 - c)

    def remote(src, dst, target):
        i = counter[0]
        counter[0] += 1
        copy = pltpu.make_async_remote_copy(
            src_ref=src, dst_ref=dst, send_sem=send.at[i], recv_sem=recv.at[i],
            device_id=target, device_id_type=MESH)
        copy.start()
        started.append(copy)
        return copy

    barrier = pltpu.get_barrier_semaphore()
    partners = [("x", k) for k in range(1, NX)] + [("y", k) for k in range(1, NY)]
    partners += [("z", k) for k in range(1, NZ)] + [("c", 1)]
    for axis, k in partners:
        pl.semaphore_signal(barrier, inc=1, device_id=to(axis, k), device_id_type=MESH)

    def strip(half, core):
        return pl.ds(pl.multiple_of(half * 4096 + core * 2048, 2048), 2048)

    own = []
    for half in range(2):
        own.append(pltpu.make_async_copy(
            inputs.at[:, :, strip(half, c)], xs.at[0, :, :, pl.ds(half * 2048, 2048)], local.at[half]))
    own.append(pltpu.make_async_copy(cot, cs.at[0], local.at[2]))
    for copy in own:
        copy.start()
    wcopy = pltpu.make_async_copy(weight, ws.at[y, z, x], local.at[3])
    wcopy.start()

    pl.semaphore_wait(barrier, len(partners))

    g1ab = [remote(weight.at[PART_AB], ws.at[(y, z, x) + PART_AB], to("z", k)) for k in range(1, NZ)]
    g1c = [remote(weight.at[PART_C], ws.at[(y, z, x) + PART_C], to("x", k)) for k in range(1, NX)]
    pair = [remote(cot, cs.at[1], to("c", 1))]
    for half in range(2):
        pair.append(remote(inputs.at[:, :, strip(half, 1 - c)],
                           xs.at[1, :, :, pl.ds(half * 2048, 2048)], to("c", 1)))

    def received(copies):
        for copy in copies:
            copy.wait_recv()

    wcopy.wait()
    received(g1c)
    ref = ws.at[(y, z, ALL) + PART_C]
    g2c = [remote(ref, ref, to("y", k)) for k in range(1, NY)]
    received(g1ab)
    ref = ws.at[(y, ALL, x) + PART_A]
    g2a = [remote(ref, ref, to("y", k)) for k in range(1, NY)]
    ref = ws.at[(y, ALL, x) + PART_B]
    g2b = [remote(ref, ref, to("x", k)) for k in range(1, NX)]

    for copy in own:
        copy.wait()
    received(pair)

    def gradient(yy):
        @pl.loop(0, 2)
        def _(h):
            start = pl.multiple_of(yy * 1024 + h * 512, 512)
            left = xs[:, :, :, pl.ds(start, 512)].reshape(512, 512)
            right = cs[...].reshape(512, 512)
            out = lax.dot_general(left, right, (((0,), (0,)), ((), ())), preferred_element_type=F32)
            grad[yy, pl.ds(h * 4, 4)] = out.reshape(4, NX, ROWS, 512)

    d = 1 - 2 * c

    def ga(k):
        return grad.at[(ALL, ALL, px(k)) + PART_A]

    def gb(k):
        return grad.at[(py(k), ALL, ALL) + PART_B]

    def gc(k):
        return grad.at[(ALL, pz(k), ALL) + PART_C]

    gradient(py(2))
    b_far = remote(gb(2), rb1.at[0], to("y", d))
    gradient(py(-d))
    b_near = remote(gb(-d), rb1.at[1], to("y", -d))
    gradient(py(d))
    gradient(y)
    a_far = remote(ga(2), ra1.at[0], to("x", d))
    c_up = [remote(gc(4), rc1.at[0], to("z", d))]
    c_down = [remote(gc(-3 * d), rc1.at[4], to("z", -d))]
    a_near = remote(ga(-d), ra1.at[1], to("x", -d))

    received(g2c)
    def wc(k):
        return ws.at[(ALL, pz(k), ALL) + PART_C]
    def wa(k):
        return ws.at[(ALL, ALL, px(k)) + PART_A]
    def wb(k):
        return ws.at[(py(k), ALL, ALL) + PART_B]
    g3c_up = [remote(wc(0), wc(0), to("z", d))]
    g3c_down = [remote(wc(0), wc(0), to("z", -d))]
    received(g2a)
    g3a_up = [remote(wa(0), wa(0), to("x", d))]
    g3a_down = [remote(wa(0), wa(0), to("x", -d))]
    received(g2b)
    g3b_up = [remote(wb(0), wb(0), to("y", d))]
    g3b_down = [remote(wb(0), wb(0), to("y", -d))]

    def add_a(k, terms):
        xx = px(k)

        @pl.loop(0, NY)
        def _(i):
            total = grad[(i, ALL, xx) + PART_A]
            for t in terms:
                total = total + ra1[t, i]
            grad[(i, ALL, xx) + PART_A] = total

    def add_b(k, terms):
        yy = py(k)

        @pl.loop(0, NX)
        def _(i):
            total = grad[(yy, ALL, i) + PART_B]
            for t in terms:
                total = total + rb1[t, :, i]
            grad[(yy, ALL, i) + PART_B] = total

    def add_c(k, terms):
        zz = pz(k)

        @pl.loop(0, NY)
        def _(i):
            total = grad[(i, zz, ALL) + PART_C]
            for t in terms:
                total = total + rc1[t, i]
            grad[(i, zz, ALL) + PART_C] = total

    def step_c(i):
        c_up[-1].wait_recv()
        add_c((4 - i) * d, [i - 1])
        c_up.append(remote(gc((4 - i) * d), rc1.at[i], to("z", d)))
        if i < 3:
            c_down[-1].wait_recv()
            add_c(-(3 - i) * d, [3 + i])
            c_down.append(remote(gc(-(3 - i) * d), rc1.at[4 + i], to("z", -d)))

    def forward_c(i):
        g3c_up[-1].wait_recv()
        g3c_up.append(remote(wc(-i * d), wc(-i * d), to("z", d)))
        if i < 3:
            g3c_down[-1].wait_recv()
            g3c_down.append(remote(wc(i * d), wc(i * d), to("z", -d)))

    step_c(1)
    b_far.wait_recv()
    add_b(d, [0])
    b_last = remote(gb(d), rb1.at[2], to("y", d))
    step_c(2)
    a_far.wait_recv()
    add_a(d, [0])
    a_last = remote(ga(d), ra1.at[2], to("x", d))
    forward_c(1)
    step_c(3)
    g3a_up[-1].wait_recv()
    g3a_up.append(remote(wa(-d), wa(-d), to("x", d)))
    g3b_up[-1].wait_recv()
    g3b_up.append(remote(wb(-d), wb(-d), to("y", d)))
    forward_c(2)

    b_near.wait_recv()
    b_last.wait_recv()
    add_b(0, [1, 2])
    s2b = [remote(grad.at[(y, ALL, px(k)) + PART_B], rb2.at[k - 1], to("x", k)) for k in range(1, NX)]
    a_near.wait_recv()
    a_last.wait_recv()
    add_a(0, [1, 2])
    s2a = [remote(grad.at[(py(k), ALL, x) + PART_A], ra2.at[k - 1], to("y", k)) for k in range(1, NY)]
    c_up[-1].wait_recv()
    c_down[-1].wait_recv()
    add_c(0, [3, 6])
    s2c = [remote(grad.at[(py(k), z, ALL) + PART_C], rc2.at[k - 1], to("y", k)) for k in range(1, NY)]
    forward_c(3)

    received(s2b)
    grad[(y, ALL, x) + PART_B] = grad[(y, ALL, x) + PART_B] + (rb2[0] + rb2[1] + rb2[2])
    received(s2a)
    grad[(y, ALL, x) + PART_A] = grad[(y, ALL, x) + PART_A] + (ra2[0] + ra2[1] + ra2[2])
    s3ab = [remote(grad.at[(y, pz(k), x) + PART_AB], rab3.at[k - 1], to("z", k)) for k in range(1, NZ)]
    received(s2c)
    grad[(y, z, ALL) + PART_C] = grad[(y, z, ALL) + PART_C] + (rc2[0] + rc2[1] + rc2[2])
    s3c = [remote(grad.at[(y, z, px(k)) + PART_C], rc3.at[k - 1], to("x", k)) for k in range(1, NX)]

    for ring in (g3a_up, g3a_down, g3b_up, g3b_down):
        ring[-1].wait_recv()
    g3c_up[-1].wait_recv()
    g3c_down[-1].wait_recv()

    acc[...] = jnp.zeros_like(acc)

    @pl.loop(0, NY)
    def _(i):
        left = xs[:, :, :, pl.ds(pl.multiple_of(i * 1024, 1024), 1024)].reshape(512, 1024)
        right = ws[i].reshape(1024, 512)
        acc[...] += jnp.dot(left, right, preferred_element_type=F32).reshape(2, 2, 128, 512)

    key_pair = remote(acc.at[1], key_in, to("c", 1))

    outs = []
    for i in range(NY):
        @pl.loop(0, 2)
        def _(h):
            right = ws[i, pl.ds(h * 4, 4)].reshape(512, 512)
            out = lax.dot_general(cs[...].reshape(512, 512), right, (((1,), (1,)), ((), ())),
                                  preferred_element_type=F32).astype(BF16)
            stage[:, :, :, pl.ds(pl.multiple_of(i * 1024 + h * 512, 512), 512)] = out.reshape(2, 2, 128, 512)

        here = pl.ds(i * 1024, 1024)
        there = pl.ds(pl.multiple_of((i // 2) * 4096 + c * 2048 + (i % 2) * 1024, 1024), 1024)
        outs.append(remote(stage.at[1, :, :, here], input_grad.at[:, :, there], to("c", 1)))
        copy = pltpu.make_async_copy(stage.at[0, :, :, here], input_grad.at[:, :, there], local.at[4 + i])
        copy.start()
        own_out = copy
        outs.append(own_out)

    received(s3c)
    received(s3ab)
    rows_ab = grad[(y, z, x) + PART_AB]
    for k in range(NZ - 1):
        rows_ab = rows_ab + rab3[k]
    rows_c = grad[(y, z, x) + PART_C]
    for k in range(NX - 1):
        rows_c = rows_c + rc3[k]
    weight_grad[:, 0:384] = rows_ab * factor
    weight_grad[:, 384:512] = rows_c * factor

    key_pair.wait_recv()
    key_out[...] = (acc[0] + key_in[...]).astype(BF16)

    for i, copy in enumerate(outs):
        if i % 2 == 0:
            copy.wait_recv()
        else:
            copy.wait()
    for copy in started:
        copy.wait_send()


def local(inputs, key_weight, key_cotangent):
    any_spec = pl.BlockSpec(memory_space=pl.ANY)
    vmem_spec = pl.BlockSpec(memory_space=pltpu.VMEM)
    return pl.pallas_call(
        kernel,
        out_shape=(
            jax.ShapeDtypeStruct(key_cotangent.shape, BF16),
            jax.ShapeDtypeStruct(inputs.shape, BF16),
            jax.ShapeDtypeStruct(key_weight.shape, F32),
        ),
        in_specs=[any_spec, vmem_spec, any_spec],
        out_specs=(vmem_spec, any_spec, vmem_spec),
        scratch_shapes=[
            pltpu.VMEM((2, 2, 128, 4096), BF16),
            pltpu.VMEM((2, 2, 128, 512), BF16),
            pltpu.VMEM((NY, NZ, NX, ROWS, 512), BF16),
            pltpu.VMEM((NY, NZ, NX, ROWS, 512), F32),
            pltpu.VMEM((2, 2, 128, 512), F32),
            pltpu.VMEM((2, 128, 512), F32),
            pltpu.VMEM((2, 2, 128, 4096), BF16),
            pltpu.VMEM((3, NY, NZ, 16, 384), F32),
            pltpu.VMEM((3, NZ, NX, 16, 384), F32),
            pltpu.VMEM((7, NY, NX, 32, 128), F32),
            pltpu.VMEM((3, NZ, 16, 384), F32),
            pltpu.VMEM((3, NZ, 16, 384), F32),
            pltpu.VMEM((3, NX, 32, 128), F32),
            pltpu.VMEM((7, 32, 384), F32),
            pltpu.VMEM((3, 32, 128), F32),
            pltpu.SemaphoreType.DMA((SEMS,)),
            pltpu.SemaphoreType.DMA((SEMS,)),
            pltpu.SemaphoreType.DMA((8,)),
        ],
        compiler_params=pltpu.CompilerParams(
            collective_id=0, has_side_effects=True, vmem_limit_bytes=56 * 2**20),
        cost_estimate=pl.CostEstimate(flops=3 * 2 * 256 * 8192 * 512, bytes_accessed=9 * 2**20, transcendentals=0),
        name="key_projection",
    )(inputs, key_weight, key_cotangent)


def solution(mesh):
    tokens = P(None, ("shard", "node"), None)
    rows = P(("node", "shard"), None)
    return jax.shard_map(local, mesh=mesh, in_specs=(tokens, rows, tokens),
                         out_specs=(tokens, tokens, rows), check_vma=False)
```

time: 647 us -> 92 us (0.14)
  the two profiles are of different devices: /device:TPU:8 before, /device:TPU:1 now
where the time goes in v1:
time: 92 us; the launch traced here: 91.8 us
  Pallas kernels  84.2 us (92%)
  local copies, waits for them, and re-layouts  6.97 us (8%)
    pallas_call x1, Pallas kernels, local(): pl.pallas_call(kernel, out_shape=(jax.ShapeDtypeStruct(key_cotangent.shap...  84.2 us
    unnamed x5, local copies, waits for them, and re-layouts  6.97 us

profile of v1, /device:TPU:1, one launch (start us, length us, event | category | flops | bytes accessed | tf_op | source)
XLA Modules:
  0.0 91.8 jit_solution(9707199476779776168)
XLA Ops:
  0.6 84.2 %key_projection.1 = (bf16[2,128,512]{2,1,0:T(8,128)(2,1)}, bf16[2,128,8192]{2,1,0:T(8,128)(2,1)}, f32[32,512]{1,0:T(8,128)}) custom-call(bf16[2,128,8192]{2,1,0:T(8,128)(2,1)} %inputs.1, bf16[32,512]{1,0:T(8,128)(2,1)} %weight.1, bf16[2,128,512]{2,1,0:T(8,128)(2,1)} %cot.1), custom_call_target="tpu_custom_call" | custom-call | flops 6442450944 | bytes 9437184 | tf_op jit(solution)/shard_map/key_projection/pallas_call | solution.py:311
  84.8 1.7 %copy.9 = bf16[2,128,512]{2,1,0:T(8,128)(2,1)} copy(bf16[2,128,512]{2,1,0:T(8,128)(2,1)} %get-tuple-element.6) | data formatting | bytes 524288
  86.5 0.0 copy-start
  86.5 4.7 %copy.10 = bf16[2,128,8192]{2,1,0:T(8,128)(2,1)} copy(bf16[2,128,8192]{2,1,0:T(8,128)(2,1)} %get-tuple-element.7) | data formatting | bytes 8388608
  91.2 0.0 copy-done
  91.2 0.6 copy.11
Async XLA Ops:
  86.5 4.7 %copy-start = (f32[32,512]{1,0:T(8,128)S(1)}, f32[32,512]{1,0:T(8,128)}, u32[]{:S(2)}) copy-start(f32[32,512]{1,0:T(8,128)} %get-tuple-element.8) | copy-start | bytes 196612

commit v2 on v1

--- a/solution.py
+++ b/solution.py
@@ -34,10 +34,24 @@
 
 SEMS = 128
 
+SCALE = 2.0 ** 8
+
+
+def encode(value):
+    square = value * value
+    return ((value * jnp.abs(value)) * (square * SCALE ** 4)).astype(BF16)
+
+
+def decode(code):
+    power = code.astype(F32)
+    root = lax.rsqrt(lax.rsqrt(jnp.abs(power))) * (1.0 / SCALE)
+    return jnp.where(power < 0, -root, root)
+
 
 def kernel(inputs, weight, cot, key_out, input_grad, weight_grad,
            xs, cs, ws, grad, acc, key_in, stage,
            ra1, rb1, rc1, ra2, rb2, rc2, rab3, rc3,
+           ea1, eb1, ec1, ea2, eb2, ec2,
            send, recv, local):
     x, y, z, c = place()
     factor = 1.0 / 256.0
@@ -129,25 +143,43 @@
 
     d = 1 - 2 * c
 
-    def ga(k):
-        return grad.at[(ALL, ALL, px(k)) + PART_A]
-
-    def gb(k):
-        return grad.at[(py(k), ALL, ALL) + PART_B]
-
-    def gc(k):
-        return grad.at[(ALL, pz(k), ALL) + PART_C]
+    def code_a(k, slot):
+        xx = px(k)
+
+        @pl.loop(0, NY)
+        def _(i):
+            ea1[slot, i] = encode(grad[(i, ALL, xx) + PART_A])
+
+        return ea1.at[slot]
+
+    def code_b(k, slot):
+        yy = py(k)
+
+        @pl.loop(0, NX)
+        def _(i):
+            eb1[slot, :, i] = encode(grad[(yy, ALL, i) + PART_B])
+
+        return eb1.at[slot]
+
+    def code_c(k, slot):
+        zz = pz(k)
+
+        @pl.loop(0, NY)
+        def _(i):
+            ec1[slot, i] = encode(grad[(i, zz, ALL) + PART_C])
+
+        return ec1.at[slot]
 
     gradient(py(2))
-    b_far = remote(gb(2), rb1.at[0], to("y", d))
+    b_far = remote(code_b(2, 0), rb1.at[0], to("y", d))
     gradient(py(-d))
-    b_near = remote(gb(-d), rb1.at[1], to("y", -d))
+    b_near = remote(code_b(-d, 1), rb1.at[1], to("y", -d))
     gradient(py(d))
     gradient(y)
-    a_far = remote(ga(2), ra1.at[0], to("x", d))
-    c_up = [remote(gc(4), rc1.at[0], to("z", d))]
-    c_down = [remote(gc(-3 * d), rc1.at[4], to("z", -d))]
-    a_near = remote(ga(-d), ra1.at[1], to("x", -d))
+    a_far = remote(code_a(2, 0), ra1.at[0], to("x", d))
+    c_up = [remote(code_c(4, 0), rc1.at[0], to("z", d))]
+    c_down = [remote(code_c(-3 * d, 4), rc1.at[4], to("z", -d))]
+    a_near = remote(code_a(-d, 1), ra1.at[1], to("x", -d))
 
     received(g2c)
     def wc(k):
@@ -172,7 +204,7 @@
         def _(i):
             total = grad[(i, ALL, xx) + PART_A]
             for t in terms:
-                total = total + ra1[t, i]
+                total = total + decode(ra1[t, i])
             grad[(i, ALL, xx) + PART_A] = total
 
     def add_b(k, terms):
@@ -182,7 +214,7 @@
         def _(i):
             total = grad[(yy, ALL, i) + PART_B]
             for t in terms:
-                total = total + rb1[t, :, i]
+                total = total + decode(rb1[t, :, i])
             grad[(yy, ALL, i) + PART_B] = total
 
     def add_c(k, terms):
@@ -192,17 +224,17 @@
         def _(i):
             total = grad[(i, zz, ALL) + PART_C]
             for t in terms:
-                total = total + rc1[t, i]
+                total = total + decode(rc1[t, i])
             grad[(i, zz, ALL) + PART_C] = total
 
     def step_c(i):
         c_up[-1].wait_recv()
         add_c((4 - i) * d, [i - 1])
-        c_up.append(remote(gc((4 - i) * d), rc1.at[i], to("z", d)))
+        c_up.append(remote(code_c((4 - i) * d, i), rc1.at[i], to("z", d)))
         if i < 3:
             c_down[-1].wait_recv()
             add_c(-(3 - i) * d, [3 + i])
-            c_down.append(remote(gc(-(3 - i) * d), rc1.at[4 + i], to("z", -d)))
+            c_down.append(remote(code_c(-(3 - i) * d, 4 + i), rc1.at[4 + i], to("z", -d)))
 
     def forward_c(i):
         g3c_up[-1].wait_recv()
@@ -214,11 +246,11 @@
     step_c(1)
     b_far.wait_recv()
     add_b(d, [0])
-    b_last = remote(gb(d), rb1.at[2], to("y", d))
+    b_last = remote(code_b(d, 2), rb1.at[2], to("y", d))
     step_c(2)
     a_far.wait_recv()
     add_a(d, [0])
-    a_last = remote(ga(d), ra1.at[2], to("x", d))
+    a_last = remote(code_a(d, 2), ra1.at[2], to("x", d))
     forward_c(1)
     step_c(3)
     g3a_up[-1].wait_recv()
@@ -230,24 +262,33 @@
     b_near.wait_recv()
     b_last.wait_recv()
     add_b(0, [1, 2])
-    s2b = [remote(grad.at[(y, ALL, px(k)) + PART_B], rb2.at[k - 1], to("x", k)) for k in range(1, NX)]
+    s2b = []
+    for k in range(1, NX):
+        eb2[k - 1] = encode(grad[(y, ALL, px(k)) + PART_B])
+        s2b.append(remote(eb2.at[k - 1], rb2.at[k - 1], to("x", k)))
     a_near.wait_recv()
     a_last.wait_recv()
     add_a(0, [1, 2])
-    s2a = [remote(grad.at[(py(k), ALL, x) + PART_A], ra2.at[k - 1], to("y", k)) for k in range(1, NY)]
+    s2a = []
+    for k in range(1, NY):
+        ea2[k - 1] = encode(grad[(py(k), ALL, x) + PART_A])
+        s2a.append(remote(ea2.at[k - 1], ra2.at[k - 1], to("y", k)))
     c_up[-1].wait_recv()
     c_down[-1].wait_recv()
     add_c(0, [3, 6])
-    s2c = [remote(grad.at[(py(k), z, ALL) + PART_C], rc2.at[k - 1], to("y", k)) for k in range(1, NY)]
+    s2c = []
+    for k in range(1, NY):
+        ec2[k - 1] = encode(grad[(py(k), z, ALL) + PART_C])
+        s2c.append(remote(ec2.at[k - 1], rc2.at[k - 1], to("y", k)))
     forward_c(3)
 
     received(s2b)
-    grad[(y, ALL, x) + PART_B] = grad[(y, ALL, x) + PART_B] + (rb2[0] + rb2[1] + rb2[2])
+    grad[(y, ALL, x) + PART_B] = grad[(y, ALL, x) + PART_B] + (decode(rb2[0]) + decode(rb2[1]) + decode(rb2[2]))
     received(s2a)
-    grad[(y, ALL, x) + PART_A] = grad[(y, ALL, x) + PART_A] + (ra2[0] + ra2[1] + ra2[2])
+    grad[(y, ALL, x) + PART_A] = grad[(y, ALL, x) + PART_A] + (decode(ra2[0]) + decode(ra2[1]) + decode(ra2[2]))
     s3ab = [remote(grad.at[(y, pz(k), x) + PART_AB], rab3.at[k - 1], to("z", k)) for k in range(1, NZ)]
     received(s2c)
-    grad[(y, z, ALL) + PART_C] = grad[(y, z, ALL) + PART_C] + (rc2[0] + rc2[1] + rc2[2])
+    grad[(y, z, ALL) + PART_C] = grad[(y, z, ALL) + PART_C] + (decode(rc2[0]) + decode(rc2[1]) + decode(rc2[2]))
     s3c = [remote(grad.at[(y, z, px(k)) + PART_C], rc3.at[k - 1], to("x", k)) for k in range(1, NX)]
 
     for ring in (g3a_up, g3a_down, g3b_up, g3b_down):
@@ -325,20 +366,26 @@
             pltpu.VMEM((2, 2, 128, 512), F32),
             pltpu.VMEM((2, 128, 512), F32),
             pltpu.VMEM((2, 2, 128, 4096), BF16),
-            pltpu.VMEM((3, NY, NZ, 16, 384), F32),
-            pltpu.VMEM((3, NZ, NX, 16, 384), F32),
-            pltpu.VMEM((7, NY, NX, 32, 128), F32),
-            pltpu.VMEM((3, NZ, 16, 384), F32),
-            pltpu.VMEM((3, NZ, 16, 384), F32),
-            pltpu.VMEM((3, NX, 32, 128), F32),
+            pltpu.VMEM((3, NY, NZ, 16, 384), BF16),
+            pltpu.VMEM((3, NZ, NX, 16, 384), BF16),
+            pltpu.VMEM((7, NY, NX, 32, 128), BF16),
+            pltpu.VMEM((3, NZ, 16, 384), BF16),
+            pltpu.VMEM((3, NZ, 16, 384), BF16),
+            pltpu.VMEM((3, NX, 32, 128), BF16),
             pltpu.VMEM((7, 32, 384), F32),
             pltpu.VMEM((3, 32, 128), F32),
+            pltpu.VMEM((3, NY, NZ, 16, 384), BF16),
+            pltpu.VMEM((3, NZ, NX, 16, 384), BF16),
+            pltpu.VMEM((7, NY, NX, 32, 128), BF16),
+            pltpu.VMEM((3, NZ, 16, 384), BF16),
+            pltpu.VMEM((3, NZ, 16, 384), BF16),
+            pltpu.VMEM((3, NX, 32, 128), BF16),
             pltpu.SemaphoreType.DMA((SEMS,)),
             pltpu.SemaphoreType.DMA((SEMS,)),
             pltpu.SemaphoreType.DMA((8,)),
         ],
         compiler_params=pltpu.CompilerParams(
-            collective_id=0, has_side_effects=True, vmem_limit_bytes=56 * 2**20),
+            collective_id=0, has_side_effects=True, vmem_limit_bytes=47 * 2**20),
         cost_estimate=pl.CostEstimate(flops=3 * 2 * 256 * 8192 * 512, bytes_accessed=9 * 2**20, transcendentals=0),
         name="key_projection",
     )(inputs, key_weight, key_cotangent)

time: 92 us -> 70.2 us (0.76)
  Pallas kernels: 84.2 us -> 64.4 us
  local copies, waits for them, and re-layouts: 6.97 us -> 5.05 us
    pallas_call x1, Pallas kernels: 84.2 us -> 64.4 us  [local(): pl.pallas_call(kernel, out_shape=(jax.ShapeDtypeStruct(key_cotangent.shap...]
    unnamed x5 -> x7, local copies, waits for them, and re-layouts: 6.97 us -> 5.05 us
where the time goes in v2:
time: 70.2 us; the launch traced here: 70 us
  Pallas kernels  64.4 us (92%)
  local copies, waits for them, and re-layouts  5.05 us (7%)
    pallas_call x1, Pallas kernels, local(): pl.pallas_call(kernel, out_shape=(jax.ShapeDtypeStruct(key_cotangent.shap...  64.4 us
    unnamed x7, local copies, waits for them, and re-layouts  5.05 us

profile of v2, /device:TPU:1, one launch (start us, length us, event | category | flops | bytes accessed | tf_op | source)
XLA Modules:
  0.0 70.0 jit_solution(4663603378525858308)
XLA Ops:
  0.6 0.0 copy-start
  0.6 0.9 %copy-done = bf16[2,128,512]{2,1,0:T(8,128)(2,1)S(1)} copy-done((bf16[2,128,512]{2,1,0:T(8,128)(2,1)S(1)}, bf16[2,128,512]{2,1,0:T(8,128)(2,1)}, u32[]{:S(2)}) %copy-start) | copy-done | bytes 262168
  1.6 0.0 copy-start.1
  1.6 0.8 %copy-done.1 = bf16[32,512]{1,0:T(8,128)(2,1)S(1)} copy-done((bf16[32,512]{1,0:T(8,128)(2,1)S(1)}, bf16[32,512]{1,0:T(8,128)(2,1)}, u32[]{:S(2)}) %copy-start.1) | copy-done | bytes 32792
  2.3 64.4 %key_projection.1 = (bf16[2,128,512]{2,1,0:T(8,128)(2,1)S(1)}, bf16[2,128,8192]{2,1,0:T(8,128)(2,1)S(1)}, f32[32,512]{1,0:T(8,128)S(1)}) custom-call(bf16[2,128,8192]{2,1,0:T(8,128)(2,1)} %inputs.1, bf16[32,512]{1,0:T(8,128)(2,1)S(1)} %copy-done.1, bf16[2,128,512]{2,1,0:T(8,128)(2,1)S(1)} %copy-done), custom_call_target="tpu_custom_call" | custom-call | flops 6442450944 | bytes 9437184 | tf_op jit(solution)/shard_map/key_projection/pallas_call | solution.py:352
  66.7 0.7 %copy.9 = bf16[2,128,512]{2,1,0:T(8,128)(2,1)} copy(bf16[2,128,512]{2,1,0:T(8,128)(2,1)S(1)} %get-tuple-element.6) | data formatting | bytes 524288
  67.4 2.0 %copy.10 = bf16[2,128,8192]{2,1,0:T(8,128)(2,1)} copy(bf16[2,128,8192]{2,1,0:T(8,128)(2,1)S(1)} %get-tuple-element.7) | data formatting | bytes 8388608
  69.4 0.6 copy.11
Async XLA Ops:
  0.6 1.0 %copy-start = (bf16[2,128,512]{2,1,0:T(8,128)(2,1)S(1)}, bf16[2,128,512]{2,1,0:T(8,128)(2,1)}, u32[]{:S(2)}) copy-start(bf16[2,128,512]{2,1,0:T(8,128)(2,1)} %cot.1) | copy-start | bytes 786436
  1.6 0.8 %copy-start.1 = (bf16[32,512]{1,0:T(8,128)(2,1)S(1)}, bf16[32,512]{1,0:T(8,128)(2,1)}, u32[]{:S(2)}) copy-start(bf16[32,512]{1,0:T(8,128)(2,1)} %weight.1) | copy-start | bytes 98308

commit v3 on v0

v3 whole, which is shorter than its diff:
```python
import functools

import jax
import jax.numpy as jnp
from jax import lax
from jax.experimental import pallas as pl
from jax.experimental.pallas import tpu as pltpu
from jax.sharding import PartitionSpec as P

MESH = pl.DeviceIdType.MESH
F32 = jnp.float32
BF16 = jnp.bfloat16
ALL = slice(None)

NX, NY, NZ = 4, 4, 8
ROWS = 32


def place():
    s = lax.axis_index("shard")
    n = lax.axis_index("node")
    x = lax.rem(s, NX)
    z = lax.rem(s // NX, NZ)
    y = (n // 2) * 2 + s // (NX * NZ)
    return x, y, z, lax.rem(n, 2)


def device(x, y, z, c):
    return (lax.rem(y, 2) * (NX * NZ) + z * NX + x, (y // 2) * 2 + c)


PART_A = (pl.ds(0, 16), pl.ds(0, 384))
PART_B = (pl.ds(16, 16), pl.ds(0, 384))
PART_AB = (pl.ds(0, 32), pl.ds(0, 384))
PART_C = (pl.ds(0, 32), pl.ds(384, 128))

SEMS = 176

SCALE = 2.0 ** 8


def encode(value):
    square = value * value
    return ((value * jnp.abs(value)) * (square * SCALE ** 4)).astype(BF16)


def decode(code):
    power = code.astype(F32)
    root = lax.rsqrt(lax.rsqrt(jnp.abs(power))) * (1.0 / SCALE)
    return jnp.where(power < 0, -root, root)


ORDER = (
    "start", "hC", "m0", "hA", "uC01", "gC1", "m1", "m2", "hB", "dC01", "m3", "uC11", "uA01", "rA0",
    "rB0", "gC2", "c21", "c01", "rB3", "rB1", "rB2", "gC3", "c11", "uC02", "rA1", "c31", "gB1",
    "c22", "dC02", "gA1", "c02", "dC11", "uC21", "c12", "uC12", "uC31", "fB0", "rA3", "uC22", "rA2",
    "gA2", "dC12", "c23", "fA0", "c32", "gB3", "c03", "uA11", "fB1", "uC03", "uC32", "c13", "fA1",
    "gB2", "dC21", "uC13", "fB3", "dC31", "fA3", "c33", "fC0", "fA2", "fB2", "uB01", "gA3", "uB11",
    "dC22", "uA21", "k0", "i0", "uC33", "dC32", "uC23", "uB31", "fC3", "k1", "uB21", "fC1", "sB",
    "fC2", "uA31", "sA", "t", "i1", "k2", "i2", "k3", "sC", "i3", "end", "z",
)


def kernel(inputs, weight, cot, key_out, input_grad, weight_grad,
           xs, cs, ws, grad, acc, key_in, stage,
           ra1, rb1, rc1, ra2, rb2, rc2, rab3, rc3,
           ea1, eb1, ec1, ea2, eb2, ec2, eab3, ec3,
           send, recv, local):
    x, y, z, c = place()
    d = 1 - 2 * c
    factor = 1.0 / 256.0

    def px(k):
        return lax.rem(x + k + 4 * NX, NX)

    def py(k):
        return lax.rem(y + k + 4 * NY, NY)

    def pz(k):
        return lax.rem(z + k + 4 * NZ, NZ)

    def to(axis, k):
        if axis == "x":
            return device(px(k), y, z, c)
        if axis == "y":
            return device(x, py(k), z, c)
        if axis == "z":
            return device(x, y, pz(k), c)
        return device(x, y, z, 1 - c)

    axes = {"A": ("x", "y", "z"), "B": ("y", "x", "z"), "C": ("z", "y", "x")}
    at_axis = {"x": px, "y": py, "z": pz}

    def at(part, first, second, third=ALL):
        first = at_axis[axes[part][0]](first)
        second = at_axis[axes[part][1]](second)
        if part == "A":
            return (second, third, first) + PART_A
        if part == "B":
            return (first, third, second) + PART_B
        return (second, first, third) + PART_C

    codes1 = {"A": ea1, "B": eb1, "C": ec1}
    codes2 = {"A": ea2, "B": eb2, "C": ec2}
    came1 = {"A": ra1, "B": rb1, "C": rc1}
    came2 = {"A": ra2, "B": rb2, "C": rc2}

    away = (2, -d, d, 0)
    behind = (0, d, -d, 2)

    copies = {}
    waited = set()

    def remote(name, src, dst, target):
        i = len(copies)
        copy = pltpu.make_async_remote_copy(
            src_ref=src, dst_ref=dst, send_sem=send.at[i], recv_sem=recv.at[i],
            device_id=target, device_id_type=MESH)
        copy.start()
        copies[name] = copy

    def arrived(*names):
        for name in names:
            if name not in waited:
                waited.add(name)
                copies[name].wait_recv()

    barrier = pltpu.get_barrier_semaphore()
    partners = [("x", k) for k in range(1, NX)] + [("y", k) for k in range(1, NY)]
    partners += [("z", k) for k in range(1, NZ)] + [("c", 1)]
    for axis, k in partners:
        pl.semaphore_signal(barrier, inc=1, device_id=to(axis, k), device_id_type=MESH)

    def strip(yy, core):
        return pl.ds(pl.multiple_of((yy // 2) * 4096 + core * 2048 + lax.rem(yy, 2) * 1024, 1024), 1024)

    def columns(yy):
        return pl.ds(pl.multiple_of(yy * 1024, 1024), 1024)

    own = [pltpu.make_async_copy(cot, cs.at[0], local.at[4])]
    for j in range(4):
        yy = py(away[j])
        own.append(pltpu.make_async_copy(inputs.at[:, :, strip(yy, c)], xs.at[0, :, :, columns(yy)], local.at[j]))
    for copy in own:
        copy.start()
    own_weight = pltpu.make_async_copy(weight, ws.at[y, z, x], local.at[5])
    own_weight.start()
    pl.semaphore_wait(barrier, len(partners))

    def start():
        for k in range(1, NX):
            remote(f"C1{k}", weight.at[PART_C], ws.at[(y, z, x) + PART_C], to("x", k))
        for k in range(1, NZ):
            remote(f"AB1{k}", weight.at[PART_AB], ws.at[(y, z, x) + PART_AB], to("z", k))
        remote("cot", cot, cs.at[1], to("c", 1))
        for j in range(4):
            yy = py((2, d, -d, 0)[j])
            remote(f"in{j}", inputs.at[:, :, strip(yy, 1 - c)], xs.at[1, :, :, columns(yy)], to("c", 1))

    def ring_start(part, j):
        axis = axes[part][0]
        ref = ws.at[at(part, 0, -behind[j])]
        remote(f"u{part}{j}0", ref, ref, to(axis, d))
        remote(f"d{part}{j}0", ref, ref, to(axis, -d))

    def head(part):
        if "weight" not in waited:
            waited.add("weight")
            own_weight.wait()
        if part == "C":
            arrived(*[f"C1{k}" for k in range(1, NX)])
        else:
            arrived(*[f"AB1{k}" for k in range(1, NZ)])
        ref = ws.at[at(part, 0, 0)]
        for j in (1, 2):
            remote(f"{part}2{j}", ref, ref, to(axes[part][1], behind[j]))
        ring_start(part, 0)

    def piece(part, j):
        arrived(f"{part}2{j}")
        if j == 1:
            ref = ws.at[at(part, 0, -d)]
            remote(f"{part}23", ref, ref, to(axes[part][1], d))
        ring_start(part, j)

    def hop(way, part, j, i):
        arrived(f"{way}{part}{j}{i - 1}")
        sign = d if way == "u" else -d
        ref = ws.at[at(part, -i * sign, -behind[j])]
        remote(f"{way}{part}{j}{i}", ref, ref, to(axes[part][0], sign))

    def gradient(j):
        if j == 0:
            own[0].wait()
            arrived("cot")
        own[1 + j].wait()
        arrived(f"in{j}")
        yy = py(away[j])

        @pl.loop(0, 2)
        def _(h):
            begin = pl.multiple_of(yy * 1024 + h * 512, 512)
            left = xs[:, :, :, pl.ds(begin, 512)].reshape(512, 512)
            right = cs[...].reshape(512, 512)
            out = lax.dot_general(left, right, (((0,), (0,)), ((), ())), preferred_element_type=F32)
            grad[yy, pl.ds(h * 4, 4)] = out.reshape(4, NX, ROWS, 512)

        if j < 2:
            for q in range(NX):
                total("B", (2, -d)[j], q, [], j)
        total("A", 2, j, [], 0)
        total("A", -d, j, [], 1)
        total("C", 4, j, [], 0)
        total("C", -3 * d, j, [], 4)

    ways = {"A": (d, -d, d), "B": (d, -d, d), "C": (d, d, d, d, -d, -d, -d)}

    def total(part, first, j, slots, send_slot):
        came = came1[part]

        def one(third):
            value = grad[at(part, first, away[j], third)]
            for slot in slots:
                value = value + decode(came[slot, j, third])
            if send_slot is None and j == 2:
                value = value + decode(came2[part][0, third])
            if send_slot is not None:
                codes1[part][send_slot, j, third] = encode(value)
            elif j < 3:
                codes2[part][j, third] = encode(value)
            else:
                grad[at(part, first, away[j], third)] = value

        if part == "C":
            one(ALL)
        else:
            @pl.loop(0, NZ // 4)
            def _(i):
                one(pl.ds(i * 4, 4))

        if send_slot is not None:
            remote(f"s{part}{j}{send_slot}", codes1[part].at[send_slot, j], came.at[send_slot, j],
                   to(axes[part][0], ways[part][send_slot]))
        elif j < 3:
            remote(f"v{part}{j}", codes2[part].at[j], came2[part].at[j], to(axes[part][1], (d, -d, d)[j]))

    def relay(part, j):
        arrived(f"s{part}{j}0")
        total(part, d, j, [0], 2)

    def relay_c(j, i):
        arrived(f"sC{j}{i - 1}")
        total("C", (4 - i) * d, j, [i - 1], i)
        if i < 3:
            arrived(f"sC{j}{3 + i}")
            total("C", -(3 - i) * d, j, [3 + i], 4 + i)

    def finish(part, j):
        slots = [3, 6] if part == "C" else [1, 2]
        arrived(*[f"s{part}{j}{slot}" for slot in slots])
        if j == 2:
            arrived(f"v{part}0")
        total(part, 0, j, slots, None)

    def second(part):
        arrived(f"v{part}1", f"v{part}2")
        came = came2[part]

        def one(third):
            where = at(part, 0, 0, third)
            grad[where] = grad[where] + (decode(came[1, third]) + decode(came[2, third]))

        if part == "C":
            one(ALL)
            for k in range(1, NX):
                ec3[k - 1] = encode(grad[(y, z, px(k)) + PART_C])
                remote(f"wC{k}", ec3.at[k - 1], rc3.at[k - 1], to("x", k))
        else:
            @pl.loop(0, NZ // 4)
            def _(i):
                one(pl.ds(i * 4, 4))

    def third():
        for k in range(1, NZ):
            eab3[k - 1] = encode(grad[(y, pz(k), x) + PART_AB])
            remote(f"w{k}", eab3.at[k - 1], rab3.at[k - 1], to("z", k))

    def last():
        arrived(*[f"wC{k}" for k in range(1, NX)])
        rows_c = grad[(y, z, x) + PART_C]
        for k in range(NX - 1):
            rows_c = rows_c + decode(rc3[k])
        weight_grad[:, 384:512] = rows_c * factor
        arrived(*[f"w{k}" for k in range(1, NZ)])
        rows_ab = grad[(y, z, x) + PART_AB]
        for k in range(NZ - 1):
            rows_ab = rows_ab + decode(rab3[k])
        weight_grad[:, 0:384] = rows_ab * factor

    def gathered(j):
        arrived(*[f"uA{j}{i}" for i in range(2)], f"dA{j}0")
        arrived(*[f"uC{j}{i}" for i in range(4)], *[f"dC{j}{i}" for i in range(3)])
        if j == 3:
            arrived(*[f"uB{q}1" for q in range(4)])
        elif j > 0:
            arrived(*[f"{' ud'[j]}B{q}0" for q in range(4)])

    def keys(j):
        gathered(j)
        yy = py(-behind[j])
        left = xs[:, :, :, columns(yy)].reshape(512, 1024)
        out = jnp.dot(left, ws[yy].reshape(1024, 512), preferred_element_type=F32).reshape(2, 2, 128, 512)
        if j == 0:
            acc[...] = out
        else:
            acc[...] += out
        if j == 3:
            remote("key", acc.at[1], key_in, to("c", 1))

    outs = []

    def back(j):
        gathered(j)
        yy = py(-behind[j])

        @pl.loop(0, 2)
        def _(h):
            right = ws[yy, pl.ds(h * 4, 4)].reshape(512, 512)
            out = lax.dot_general(cs[...].reshape(512, 512), right, (((1,), (1,)), ((), ())),
                                  preferred_element_type=F32).astype(BF16)
            stage[:, :, :, pl.ds(pl.multiple_of(j * 1024 + h * 512, 512), 512)] = out.reshape(2, 2, 128, 512)

        here = pl.ds(j * 1024, 1024)
        there = strip(yy, c)
        remote(f"out{j}", stage.at[1, :, :, here], input_grad.at[:, :, there], to("c", 1))
        copy = pltpu.make_async_copy(stage.at[0, :, :, here], input_grad.at[:, :, there], local.at[6 + j])
        copy.start()
        outs.append(copy)

    def close():
        arrived("key")
        key_out[...] = (acc[0] + key_in[...]).astype(BF16)
        for copy in outs:
            copy.wait()
        arrived(*[f"out{j}" for j in range(NY)])
        for copy in copies.values():
            copy.wait_send()

    steps = {"start": start, "t": third, "end": last, "z": close}
    for part in "ABC":
        steps[f"h{part}"] = functools.partial(head, part)
        steps[f"s{part}"] = functools.partial(second, part)
        for j in range(4):
            steps[f"g{part}{j}"] = functools.partial(piece, part, j)
            steps[f"r{part}{j}"] = functools.partial(relay, part, j)
            steps[f"f{part}{j}"] = functools.partial(finish, part, j)
            for i in range(1, 4):
                steps[f"u{part}{j}{i}"] = functools.partial(hop, "u", part, j, i)
                steps[f"d{part}{j}{i}"] = functools.partial(hop, "d", part, j, i)
    for j in range(4):
        steps[f"m{j}"] = functools.partial(gradient, j)
        steps[f"k{j}"] = functools.partial(keys, j)
        steps[f"i{j}"] = functools.partial(back, j)
        for i in range(1, 4):
            steps[f"c{j}{i}"] = functools.partial(relay_c, j, i)
    for name in ORDER:
        steps[name]()


def local(inputs, key_weight, key_cotangent):
    any_spec = pl.BlockSpec(memory_space=pl.ANY)
    vmem_spec = pl.BlockSpec(memory_space=pltpu.VMEM)
    codes = [
        pltpu.VMEM((3, NY, NZ, 16, 384), BF16),
        pltpu.VMEM((3, NX, NZ, 16, 384), BF16),
        pltpu.VMEM((7, NY, NX, 32, 128), BF16),
        pltpu.VMEM((3, NZ, 16, 384), BF16),
        pltpu.VMEM((3, NZ, 16, 384), BF16),
        pltpu.VMEM((3, NX, 32, 128), BF16),
        pltpu.VMEM((7, 32, 384), BF16),
        pltpu.VMEM((3, 32, 128), BF16),
    ]
    return pl.pallas_call(
        kernel,
        out_shape=(
            jax.ShapeDtypeStruct(key_cotangent.shape, BF16),
            jax.ShapeDtypeStruct(inputs.shape, BF16),
            jax.ShapeDtypeStruct(key_weight.shape, F32),
        ),
        in_specs=[any_spec, vmem_spec, any_spec],
        out_specs=(vmem_spec, any_spec, vmem_spec),
        scratch_shapes=[
            pltpu.VMEM((2, 2, 128, 4096), BF16),
            pltpu.VMEM((2, 2, 128, 512), BF16),
            pltpu.VMEM((NY, NZ, NX, ROWS, 512), BF16),
            pltpu.VMEM((NY, NZ, NX, ROWS, 512), F32),
            pltpu.VMEM((2, 2, 128, 512), F32),
            pltpu.VMEM((2, 128, 512), F32),
            pltpu.VMEM((2, 2, 128, 4096), BF16),
            *codes,
            *codes,
            pltpu.SemaphoreType.DMA((SEMS,)),
            pltpu.SemaphoreType.DMA((SEMS,)),
            pltpu.SemaphoreType.DMA((10,)),
        ],
        compiler_params=pltpu.CompilerParams(
            collective_id=0, has_side_effects=True, vmem_limit_bytes=47 * 2**20),
        cost_estimate=pl.CostEstimate(flops=3 * 2 * 256 * 8192 * 512, bytes_accessed=9 * 2**20, transcendentals=0),
        name="key_projection",
    )(inputs, key_weight, key_cotangent)


def solution(mesh):
    tokens = P(None, ("shard", "node"), None)
    rows = P(("node", "shard"), None)
    return jax.shard_map(local, mesh=mesh, in_specs=(tokens, rows, tokens),
                         out_specs=(tokens, tokens, rows), check_vma=False)
```

time: 647 us -> 64.3 us (0.10)
  the two profiles are of different devices: /device:TPU:8 before, /device:TPU:9 now
where the time goes in v3:
time: 64.3 us; the launch traced here: 64.1 us
  Pallas kernels  58.4 us (91%)
  local copies, waits for them, and re-layouts  5.05 us (8%)
  between operations  0.65 us (1%)
    pallas_call x1, Pallas kernels, local(): pl.pallas_call(kernel, out_shape=(jax.ShapeDtypeStruct(key_cotangent.shap...  58.4 us
    unnamed x7, local copies, waits for them, and re-layouts  5.05 us

profile of v3, /device:TPU:9, one launch (start us, length us, event | category | flops | bytes accessed | tf_op | source)
XLA Modules:
  0.0 64.1 jit_solution(6409103655380418147)
XLA Ops:
  0.6 0.0 copy-start
  0.6 0.9 %copy-done = bf16[2,128,512]{2,1,0:T(8,128)(2,1)S(1)} copy-done((bf16[2,128,512]{2,1,0:T(8,128)(2,1)S(1)}, bf16[2,128,512]{2,1,0:T(8,128)(2,1)}, u32[]{:S(2)}) %copy-start) | copy-done | bytes 262168
  1.6 0.0 copy-start.1
  1.6 0.8 %copy-done.1 = bf16[32,512]{1,0:T(8,128)(2,1)S(1)} copy-done((bf16[32,512]{1,0:T(8,128)(2,1)S(1)}, bf16[32,512]{1,0:T(8,128)(2,1)}, u32[]{:S(2)}) %copy-start.1) | copy-done | bytes 32792
  2.3 58.4 %key_projection.1 = (bf16[2,128,512]{2,1,0:T(8,128)(2,1)S(1)}, bf16[2,128,8192]{2,1,0:T(8,128)(2,1)S(1)}, f32[32,512]{1,0:T(8,128)S(1)}) custom-call(bf16[2,128,8192]{2,1,0:T(8,128)(2,1)} %inputs.1, bf16[32,512]{1,0:T(8,128)(2,1)S(1)} %copy-done.1, bf16[2,128,512]{2,1,0:T(8,128)(2,1)S(1)} %copy-done), custom_call_target="tpu_custom_call" | custom-call | flops 6442450944 | bytes 9437184 | tf_op jit(solution)/shard_map/key_projection/pallas_call | solution.py:383
  60.8 0.7 %copy.9 = bf16[2,128,512]{2,1,0:T(8,128)(2,1)} copy(bf16[2,128,512]{2,1,0:T(8,128)(2,1)S(1)} %get-tuple-element.6) | data formatting | bytes 524288
  61.5 2.0 %copy.10 = bf16[2,128,8192]{2,1,0:T(8,128)(2,1)} copy(bf16[2,128,8192]{2,1,0:T(8,128)(2,1)S(1)} %get-tuple-element.7) | data formatting | bytes 8388608
  63.5 0.6 copy.11
Async XLA Ops:
  0.6 1.0 %copy-start = (bf16[2,128,512]{2,1,0:T(8,128)(2,1)S(1)}, bf16[2,128,512]{2,1,0:T(8,128)(2,1)}, u32[]{:S(2)}) copy-start(bf16[2,128,512]{2,1,0:T(8,128)(2,1)} %cot.1) | copy-start | bytes 786436
  1.6 0.8 %copy-start.1 = (bf16[32,512]{1,0:T(8,128)(2,1)S(1)}, bf16[32,512]{1,0:T(8,128)(2,1)}, u32[]{:S(2)}) copy-start(bf16[32,512]{1,0:T(8,128)(2,1)} %weight.1) | copy-start | bytes 98308

commit v4 on v3

--- a/solution.py
+++ b/solution.py
@@ -197,13 +197,10 @@
         arrived(f"in{j}")
         yy = py(away[j])
 
-        @pl.loop(0, 2)
-        def _(h):
-            begin = pl.multiple_of(yy * 1024 + h * 512, 512)
-            left = xs[:, :, :, pl.ds(begin, 512)].reshape(512, 512)
-            right = cs[...].reshape(512, 512)
-            out = lax.dot_general(left, right, (((0,), (0,)), ((), ())), preferred_element_type=F32)
-            grad[yy, pl.ds(h * 4, 4)] = out.reshape(4, NX, ROWS, 512)
+        left = xs[:, :, :, columns(yy)].reshape(512, 1024)
+        right = cs[...].reshape(512, 512)
+        out = lax.dot_general(left, right, (((0,), (0,)), ((), ())), preferred_element_type=F32)
+        grad[yy] = out.reshape(NZ, NX, ROWS, 512)
 
         if j < 2:
             for q in range(NX):
@@ -323,14 +320,10 @@
         gathered(j)
         yy = py(-behind[j])
 
-        @pl.loop(0, 2)
-        def _(h):
-            right = ws[yy, pl.ds(h * 4, 4)].reshape(512, 512)
-            out = lax.dot_general(cs[...].reshape(512, 512), right, (((1,), (1,)), ((), ())),
-                                  preferred_element_type=F32).astype(BF16)
-            stage[:, :, :, pl.ds(pl.multiple_of(j * 1024 + h * 512, 512), 512)] = out.reshape(2, 2, 128, 512)
-
         here = pl.ds(j * 1024, 1024)
+        out = lax.dot_general(cs[...].reshape(512, 512), ws[yy].reshape(1024, 512), (((1,), (1,)), ((), ())),
+                              preferred_element_type=F32).astype(BF16)
+        stage[:, :, :, here] = out.reshape(2, 2, 128, 1024)
         there = strip(yy, c)
         remote(f"out{j}", stage.at[1, :, :, here], input_grad.at[:, :, there], to("c", 1))
         copy = pltpu.make_async_copy(stage.at[0, :, :, here], input_grad.at[:, :, there], local.at[6 + j])
@@ -367,6 +360,21 @@
         steps[name]()
 
 
+WRITES = 10
+
+
+def write(key_in, grad_in, weight_in, key_out, input_grad, weight_grad, sems):
+    copies = [pltpu.make_async_copy(key_in, key_out, sems.at[0]),
+              pltpu.make_async_copy(weight_in, weight_grad, sems.at[1])]
+    for i in range(8):
+        part = (i // 4, pl.ds(i % 4 * 32, 32))
+        copies.append(pltpu.make_async_copy(grad_in.at[part], input_grad.at[part], sems.at[2 + i]))
+    for copy in copies:
+        copy.start()
+    for copy in copies:
+        copy.wait()
+
+
 def local(inputs, key_weight, key_cotangent):
     any_spec = pl.BlockSpec(memory_space=pl.ANY)
     vmem_spec = pl.BlockSpec(memory_space=pltpu.VMEM)
@@ -380,14 +388,17 @@
         pltpu.VMEM((7, 32, 384), BF16),
         pltpu.VMEM((3, 32, 128), BF16),
     ]
-    return pl.pallas_call(
+    inputs, key_weight, key_cotangent = (
+        pltpu.with_memory_space_constraint(v, pltpu.HBM) for v in (inputs, key_weight, key_cotangent))
+    hbm_spec = pl.BlockSpec(memory_space=pltpu.HBM)
+    results = pl.pallas_call(
         kernel,
         out_shape=(
             jax.ShapeDtypeStruct(key_cotangent.shape, BF16),
             jax.ShapeDtypeStruct(inputs.shape, BF16),
             jax.ShapeDtypeStruct(key_weight.shape, F32),
         ),
-        in_specs=[any_spec, vmem_spec, any_spec],
+        in_specs=[hbm_spec, hbm_spec, hbm_spec],
         out_specs=(vmem_spec, any_spec, vmem_spec),
         scratch_shapes=[
             pltpu.VMEM((2, 2, 128, 4096), BF16),
@@ -408,6 +419,16 @@
         cost_estimate=pl.CostEstimate(flops=3 * 2 * 256 * 8192 * 512, bytes_accessed=9 * 2**20, transcendentals=0),
         name="key_projection",
     )(inputs, key_weight, key_cotangent)
+    return pl.pallas_call(
+        write,
+        out_shape=[jax.ShapeDtypeStruct(r.shape, r.dtype) for r in results],
+        in_specs=[any_spec] * 3,
+        out_specs=[any_spec] * 3,
+        scratch_shapes=[pltpu.SemaphoreType.DMA((WRITES,))],
+        cost_estimate=pl.CostEstimate(flops=0, bytes_accessed=9 * 2**20, transcendentals=0),
+        compiler_params=pltpu.CompilerParams(vmem_limit_bytes=2**20),
+        name="write_results",
+    )(*results)
 
 
 def solution(mesh):

time: 64.3 us -> 60.8 us (0.946)
  the two profiles are of different devices: /device:TPU:9 before, /device:TPU:1 now
where the time goes in v4:
time: 60.8 us; the launch traced here: 60.7 us
  Pallas kernels  60.1 us (99%)
  between operations  0.64 us (1%)
    pallas_call x1, Pallas kernels, local(): pl.pallas_call(kernel, out_shape=(jax.ShapeDtypeStruct(key_cotangent.shap...  57.9 us
    pallas_call x1, Pallas kernels, local(): pl.pallas_call(write, out_shape=[jax.ShapeDtypeStruct(r.shape, r.dtype) f...  2.2 us

profile of v4, /device:TPU:1, one launch (start us, length us, event | category | flops | bytes accessed | tf_op | source)
XLA Modules:
  0.0 60.7 jit_solution(5185968880692773427)
XLA Ops:
  0.6 57.9 %key_projection.1 = (bf16[2,128,512]{2,1,0:T(8,128)(2,1)S(1)}, bf16[2,128,8192]{2,1,0:T(8,128)(2,1)S(1)}, f32[32,512]{1,0:T(8,128)S(1)}) custom-call(bf16[2,128,8192]{2,1,0:T(8,128)(2,1)} %inputs.1, bf16[32,512]{1,0:T(8,128)(2,1)} %weight.1, bf16[2,128,512]{2,1,0:T(8,128)(2,1)} %cot.1), custom_call_target="tpu_custom_call" | custom-call | flops 6442450944 | bytes 9437184 | tf_op jit(solution)/shard_map/key_projection/pallas_call | solution.py:394
  58.5 2.2 %write_results.1 = (bf16[2,128,512]{2,1,0:T(8,128)(2,1)}, bf16[2,128,8192]{2,1,0:T(8,128)(2,1)}, f32[32,512]{1,0:T(8,128)}) custom-call(bf16[2,128,512]{2,1,0:T(8,128)(2,1)S(1)} %get-tuple-element.6.key_in, bf16[2,128,8192]{2,1,0:T(8,128)(2,1)S(1)} %get-tuple-element.7.grad_in, f32[32,512]{1,0:T(8,128)S(1)} %get-tuple-element.8.weight_in), custom_call_target="tpu_custom_call" | custom-call | bytes 9437184 | tf_op jit(solution)/shard_map/write_results/pallas_call | solution.py:422

commit v5 on v4

--- a/solution.py
+++ b/solution.py
@@ -34,7 +34,7 @@
 PART_AB = (pl.ds(0, 32), pl.ds(0, 384))
 PART_C = (pl.ds(0, 32), pl.ds(384, 128))
 
-SEMS = 176
+SEMS = 192
 
 SCALE = 2.0 ** 8
 
@@ -57,7 +57,7 @@
     "gA2", "dC12", "c23", "fA0", "c32", "gB3", "c03", "uA11", "fB1", "uC03", "uC32", "c13", "fA1",
     "gB2", "dC21", "uC13", "fB3", "dC31", "fA3", "c33", "fC0", "fA2", "fB2", "uB01", "gA3", "uB11",
     "dC22", "uA21", "k0", "i0", "uC33", "dC32", "uC23", "uB31", "fC3", "k1", "uB21", "fC1", "sB",
-    "fC2", "uA31", "sA", "t", "i1", "k2", "i2", "k3", "sC", "i3", "end", "z",
+    "tB", "fC2", "uA31", "sA", "tA", "i1", "k2", "i2", "k3", "sC", "i3", "end", "z",
 )
 
 
@@ -145,13 +145,14 @@
         copy.start()
     own_weight = pltpu.make_async_copy(weight, ws.at[y, z, x], local.at[5])
     own_weight.start()
+    own_weight.wait()
     pl.semaphore_wait(barrier, len(partners))
 
     def start():
         for k in range(1, NX):
-            remote(f"C1{k}", weight.at[PART_C], ws.at[(y, z, x) + PART_C], to("x", k))
+            remote(f"C1{k}", ws.at[(y, z, x) + PART_C], ws.at[(y, z, x) + PART_C], to("x", k))
         for k in range(1, NZ):
-            remote(f"AB1{k}", weight.at[PART_AB], ws.at[(y, z, x) + PART_AB], to("z", k))
+            remote(f"AB1{k}", ws.at[(y, z, x) + PART_AB], ws.at[(y, z, x) + PART_AB], to("z", k))
         remote("cot", cot, cs.at[1], to("c", 1))
         for j in range(4):
             yy = py((2, d, -d, 0)[j])
@@ -164,9 +165,6 @@
         remote(f"d{part}{j}0", ref, ref, to(axis, -d))
 
     def head(part):
-        if "weight" not in waited:
-            waited.add("weight")
-            own_weight.wait()
         if part == "C":
             arrived(*[f"C1{k}" for k in range(1, NX)])
         else:
@@ -277,10 +275,11 @@
             def _(i):
                 one(pl.ds(i * 4, 4))
 
-    def third():
+    def third(part):
+        rows, cols = PART_A if part == "A" else PART_B
         for k in range(1, NZ):
-            eab3[k - 1] = encode(grad[(y, pz(k), x) + PART_AB])
-            remote(f"w{k}", eab3.at[k - 1], rab3.at[k - 1], to("z", k))
+            eab3[k - 1, rows] = encode(grad[y, pz(k), x, rows, cols])
+            remote(f"w{part}{k}", eab3.at[k - 1, rows], rab3.at[k - 1, rows], to("z", k))
 
     def last():
         arrived(*[f"wC{k}" for k in range(1, NX)])
@@ -288,7 +287,7 @@
         for k in range(NX - 1):
             rows_c = rows_c + decode(rc3[k])
         weight_grad[:, 384:512] = rows_c * factor
-        arrived(*[f"w{k}" for k in range(1, NZ)])
+        arrived(*[f"w{part}{k}" for part in "AB" for k in range(1, NZ)])
         rows_ab = grad[(y, z, x) + PART_AB]
         for k in range(NZ - 1):
             rows_ab = rows_ab + decode(rab3[k])
@@ -305,14 +304,16 @@
     def keys(j):
         gathered(j)
         yy = py(-behind[j])
-        left = xs[:, :, :, columns(yy)].reshape(512, 1024)
-        out = jnp.dot(left, ws[yy].reshape(1024, 512), preferred_element_type=F32).reshape(2, 2, 128, 512)
-        if j == 0:
-            acc[...] = out
-        else:
-            acc[...] += out
-        if j == 3:
-            remote("key", acc.at[1], key_in, to("c", 1))
+        right = ws[yy].reshape(1024, 512)
+        for who in (1, 0):
+            left = xs[who, :, :, columns(yy)].reshape(256, 1024)
+            out = jnp.dot(left, right, preferred_element_type=F32).reshape(2, 128, 512)
+            if j == 0:
+                acc[who] = out
+            else:
+                acc[who] += out
+            if j == 3 and who == 1:
+                remote("key", acc.at[1], key_in, to("c", 1))
 
     outs = []
 
@@ -321,11 +322,14 @@
         yy = py(-behind[j])
 
         here = pl.ds(j * 1024, 1024)
-        out = lax.dot_general(cs[...].reshape(512, 512), ws[yy].reshape(1024, 512), (((1,), (1,)), ((), ())),
-                              preferred_element_type=F32).astype(BF16)
-        stage[:, :, :, here] = out.reshape(2, 2, 128, 1024)
         there = strip(yy, c)
-        remote(f"out{j}", stage.at[1, :, :, here], input_grad.at[:, :, there], to("c", 1))
+        right = ws[yy].reshape(1024, 512)
+        for who in (1, 0):
+            out = lax.dot_general(cs[who].reshape(256, 512), right, (((1,), (1,)), ((), ())),
+                                  preferred_element_type=F32).astype(BF16)
+            stage[who, :, :, here] = out.reshape(2, 128, 1024)
+            if who == 1:
+                remote(f"out{j}", stage.at[1, :, :, here], input_grad.at[:, :, there], to("c", 1))
         copy = pltpu.make_async_copy(stage.at[0, :, :, here], input_grad.at[:, :, there], local.at[6 + j])
         copy.start()
         outs.append(copy)
@@ -339,10 +343,11 @@
         for copy in copies.values():
             copy.wait_send()
 
-    steps = {"start": start, "t": third, "end": last, "z": close}
+    steps = {"start": start, "end": last, "z": close}
     for part in "ABC":
         steps[f"h{part}"] = functools.partial(head, part)
         steps[f"s{part}"] = functools.partial(second, part)
+        steps[f"t{part}"] = functools.partial(third, part)
         for j in range(4):
             steps[f"g{part}{j}"] = functools.partial(piece, part, j)
             steps[f"r{part}{j}"] = functools.partial(relay, part, j)

time: 60.8 us -> 60.4 us (level)
  no operation moved by 1% of the time
where the time goes in v5:
time: 60.4 us; the launch traced here: 60.3 us
  Pallas kernels  59.7 us (99%)
  between operations  0.64 us (1%)
    pallas_call x1, Pallas kernels, local(): pl.pallas_call(kernel, out_shape=(jax.ShapeDtypeStruct(key_cotangent.shap...  57.5 us
    pallas_call x1, Pallas kernels, local(): pl.pallas_call(write, out_shape=[jax.ShapeDtypeStruct(r.shape, r.dtype) f...  2.2 us

profile of v5, /device:TPU:1, one launch (start us, length us, event | category | flops | bytes accessed | tf_op | source)
XLA Modules:
  0.0 60.3 jit_solution(51726925284323631)
XLA Ops:
  0.6 57.5 %key_projection.1 = (bf16[2,128,512]{2,1,0:T(8,128)(2,1)S(1)}, bf16[2,128,8192]{2,1,0:T(8,128)(2,1)S(1)}, f32[32,512]{1,0:T(8,128)S(1)}) custom-call(bf16[2,128,8192]{2,1,0:T(8,128)(2,1)} %inputs.1, bf16[32,512]{1,0:T(8,128)(2,1)} %weight.1, bf16[2,128,512]{2,1,0:T(8,128)(2,1)} %cot.1), custom_call_target="tpu_custom_call" | custom-call | flops 6442450944 | bytes 9437184 | tf_op jit(solution)/shard_map/key_projection/pallas_call | solution.py:399
  58.1 2.2 %write_results.1 = (bf16[2,128,512]{2,1,0:T(8,128)(2,1)}, bf16[2,128,8192]{2,1,0:T(8,128)(2,1)}, f32[32,512]{1,0:T(8,128)}) custom-call(bf16[2,128,512]{2,1,0:T(8,128)(2,1)S(1)} %get-tuple-element.6.key_in, bf16[2,128,8192]{2,1,0:T(8,128)(2,1)S(1)} %get-tuple-element.7.grad_in, f32[32,512]{1,0:T(8,128)S(1)} %get-tuple-element.8.weight_in), custom_call_target="tpu_custom_call" | custom-call | bytes 9437184 | tf_op jit(solution)/shard_map/write_results/pallas_call | solution.py:427
